TPU v7x, 32 devices: a whole 2x2x4 slice. The times are simulated.
32 devices in a mesh: dp: 8 (over y, x, core), space: 4 (over z).
Axes of the slice: x: 2, y: 2, z: 4, core: 2. Of those that a mesh axis runs over, the one named last changes fastest.
Arguments:
- features: bfloat16 [8, 12288, 128], P('dp', 'space'), may hold values from -6 to 6
- neighbours: int32 [8, 27, 12288], P('dp', None, 'space'), may hold values from -1 to 12287, as said below
- weight: bfloat16 [27, 128, 128], replicated, may hold values from -0.109375 to 0.109375
- grad_out: bfloat16 [8, 12288, 128], P('dp', 'space'), may hold values from -6 to 6
Outputs:
- conv_out: bfloat16 [8, 12288, 128], P('dp', 'space')
- grad_in: bfloat16 [8, 12288, 128], P('dp', 'space')
- grad_w: float32 [27, 128, 128], replicated
Inputs may be any that keep to these rules, and one draw needn't show every extreme that they name: Voxels of a scene are ordered by layer, 1024 per layer and layer z holding indices z * 1024 to (z + 1) * 1024 - 1; within a layer they are ordered by cell y * 64 + x, and every grid row y of every layer holds exactly 16 active voxels, so row y of layer z holds indices z * 1024 + y * 16 onward. An entry for offset (dz, dy, dx) of a voxel in layer z, row y points into layer z + dz, row y + dy. The map is symmetric: neighbours[26 - k, neighbours[k, i]] = i wherever neighbours[k, i] >= 0, and neighbours[13, i] = i.
All inputs are finite; a program needn't handle non-finite values.
Results may differ from a plain program's by a relative error of at most 0.0055.
Values may be sent and summed in bfloat16 or wider, within the bound.
No kernel may reach another device: no remote copies, remote signals or barrier semaphores. Data moves between devices by JAX's collectives and lax.ppermute only.
A program may use at most 64 MiB of HBM per device.

v0:
```python
import functools
import math

import jax
import jax.numpy as jnp
from jax import lax
from jax.experimental import pallas as pl
from jax.experimental.pallas import tpu as pltpu
from jax.sharding import PartitionSpec as P

PSIDE = 64
ROW = PSIDE // 4
LAYER = PSIDE * ROW
T = 128
CHUNK_W = 512
CHUNK_C = 256
VMEM_LIMIT = 28 * 1024 * 1024
CONV_VMEM_LIMIT = 58 * 1024 * 1024
VMEM = pl.BlockSpec(memory_space=pltpu.VMEM)
SMEM = pl.BlockSpec(memory_space=pltpu.SMEM)


def offset_of(k):
    return k // 9 - 1, (k // 3) % 3 - 1, k % 3 - 1


def row_in_scene_window(neighbours, shift):
    return jnp.where(neighbours >= 0, (neighbours - shift) & (T - 1), -1)


def one_hot(hit):
    return jnp.where(hit, jnp.ones((), jnp.bfloat16), jnp.zeros((), jnp.bfloat16))


def beside(xe, first, f_ref, g_ref, rows):
    channels = f_ref.shape[1]
    xe[first : first + rows, 0:channels] = f_ref[0:rows, :]
    xe[first : first + rows, channels:] = g_ref[0:rows, :]


def fill_edges(xe, shift):
    edge = jnp.zeros((ROW, xe.shape[1]), jnp.bfloat16)
    xe[0:ROW, :] = edge
    xe[xe.shape[0] - ROW :, :] = edge
    shift[...] = jnp.zeros_like(shift)
    for k in range(27):
        if offset_of(k)[1]:
            shift[k : k + 1, :] = jnp.full((1, T), ROW * offset_of(k)[1], jnp.int32)


def add_weight_terms(o, ks, source, center, f_ref, g_ref, nb_ref, xe, shift, gf, gg, acc):
    channels = f_ref.shape[1]
    spot = lax.broadcasted_iota(jnp.int32, (T, T), 1).astype(jnp.bfloat16)
    base = pl.multiple_of(o * CHUNK_W, CHUNK_W)
    pads = jnp.full((5, T), -1, jnp.int32)
    for h in range(CHUNK_W // T):
        rows = slice(h * T, (h + 1) * T)
        mine = jnp.concatenate([nb_ref[:, o * (CHUNK_W // T) + h, :], pads], axis=0)
        mine = row_in_scene_window(mine, shift[...]).T.astype(jnp.bfloat16)
        for dz, dy in sorted({offset_of(k)[:2] for k in ks}):
            some = [k for k in ks if offset_of(k)[:2] == (dz, dy)]
            start = base + (source + h * T + ROW * dy + LAYER * dz)
            window = xe[pl.ds(pl.multiple_of(start, ROW), T), :]
            hot = jnp.concatenate([one_hot(mine[:, k : k + 1] == spot) for k in some], axis=0)
            picked = jnp.dot(hot, window, preferred_element_type=jnp.float32)
            picked = picked.astype(jnp.bfloat16)
            for q, k in enumerate(some):
                part = picked[q * T : (q + 1) * T]
                gf[rows, k * T : (k + 1) * T] = part[:, :channels]
                gg[rows, k * T : (k + 1) * T] = part[:, channels:]
    here = pl.ds(base, CHUNK_W)
    if center:
        gg[:, 13 * T :] = g_ref[here, :]
    span = slice(ks[0] * T, (ks[-1] + 1) * T)
    acc[:, span] += jnp.dot(g_ref[here, :].T, gf[:, span], preferred_element_type=jnp.float32)
    last = ks[-1] + 1 + (1 if center else 0)
    span = slice(ks[0] * T, last * T)
    to = slice((13 + ks[0]) * T, (13 + last) * T)
    acc[:, to] += jnp.dot(f_ref[here, :].T, gg[:, span], preferred_element_type=jnp.float32)


def weight_inner_kernel(voxels, f_ref, g_ref, nb_ref, acc, xe, shift, gf, gg):
    beside(xe, ROW, f_ref, g_ref, voxels)
    fill_edges(xe, shift)
    acc[...] = jnp.zeros_like(acc)
    rest = (f_ref, g_ref, nb_ref, xe, shift, gf, gg, acc)

    @pl.loop(0, LAYER // CHUNK_W)
    def _(o):
        add_weight_terms(o, list(range(9, 13)), ROW, True, *rest)

    @pl.loop(LAYER // CHUNK_W, voxels // CHUNK_W)
    def _(o):
        add_weight_terms(o, list(range(13)), ROW, True, *rest)


def weight_halo_kernel(scale, parity_ref, f_ref, g_ref, low_ref, nb_ref, in_ref, mine_ref, other_ref, xe, shift, gf, gg, acc, out_ref):
    xe[ROW : ROW + LAYER, :] = low_ref[...]
    fill_edges(xe, shift)
    acc[...] = in_ref[...]
    rest = (f_ref, g_ref, nb_ref, xe, shift, gf, gg, acc)

    @pl.loop(0, LAYER // CHUNK_W)
    def _(o):
        add_weight_terms(o, list(range(9)), ROW + LAYER, False, *rest)

    for k in range(13):
        out_ref[k * T : (k + 1) * T, :] = (acc[:, k * T : (k + 1) * T].T * scale).astype(out_ref.dtype)
    for k in range(14):
        out_ref[(26 - k) * T : (27 - k) * T, :] = (
            acc[:, (13 + k) * T : (14 + k) * T] * scale
        ).astype(out_ref.dtype)
    if out_ref.shape[0] > 27 * T:
        out_ref[27 * T :, :] = jnp.zeros((out_ref.shape[0] - 27 * T, out_ref.shape[1]), out_ref.dtype)
    half = out_ref.shape[0] // 2
    parity = parity_ref[0]
    mine_ref[...] = out_ref[pl.ds(pl.multiple_of(parity * half, 16), half), :]
    other_ref[...] = out_ref[pl.ds(pl.multiple_of((1 - parity) * half, 16), half), :]


def weight_scratch(rows, channels):
    return [
        pltpu.VMEM((rows + 2 * ROW, 2 * channels), jnp.bfloat16),
        pltpu.VMEM((32, T), jnp.int32),
        pltpu.VMEM((CHUNK_W, 13 * T), jnp.bfloat16),
        pltpu.VMEM((CHUNK_W, 14 * T), jnp.bfloat16),
    ]


def grad_w_inner(feats, grads, neigh):
    voxels, channels = feats.shape
    return pl.pallas_call(
        functools.partial(weight_inner_kernel, voxels),
        out_shape=jax.ShapeDtypeStruct((channels, 27 * T), jnp.float32),
        in_specs=[VMEM] * 3,
        out_specs=VMEM,
        scratch_shapes=weight_scratch(voxels, channels),
        compiler_params=pltpu.CompilerParams(vmem_limit_bytes=VMEM_LIMIT),
        cost_estimate=pl.CostEstimate(flops=8 * 10**9, bytes_accessed=4 * 10**6, transcendentals=0),
        name="weight_gradient_inner",
    )(feats, grads, neigh)


def grad_w_halo(feats, grads, low, neigh, partial, parity, scale, rows):
    channels = feats.shape[1]
    out = jax.ShapeDtypeStruct((rows // 2, channels), jnp.bfloat16)
    return pl.pallas_call(
        functools.partial(weight_halo_kernel, scale),
        out_shape=(out, out),
        in_specs=[SMEM] + [VMEM] * 5,
        out_specs=(VMEM, VMEM),
        scratch_shapes=weight_scratch(LAYER, channels)
        + [
            pltpu.VMEM((channels, 27 * T), jnp.float32),
            pltpu.VMEM((rows, channels), jnp.bfloat16),
        ],
        compiler_params=pltpu.CompilerParams(vmem_limit_bytes=VMEM_LIMIT),
        cost_estimate=pl.CostEstimate(flops=3 * 10**9, bytes_accessed=4 * 10**6, transcendentals=0),
        name="weight_gradient_halo",
    )(parity, feats, grads, low, neigh, partial)


def rows_needed(run):
    first, end = run
    return (
        first - LAYER - (ROW if first % LAYER else 0),
        end + LAYER + (ROW if end % LAYER else 0),
    )


def conv_kernel(voxels, run, make_wt, f_ref, g_ref, nb_ref, w_hbm, *rest):
    if make_wt:
        conv_hbm, gin_hbm, wt, w_ref, *scratch = rest[-14:]
    else:
        wt_hbm = rest[0]
        conv_hbm, gin_hbm, wt, *scratch = rest[-13:]
    conv_ref, gin_ref, xe, nb, rel, gf, gg, gf2, gg2, sems = scratch
    halos = list(rest[(0 if make_wt else 3) :])
    channels = f_ref.shape[1]
    size = run[1] - run[0]

    origin = run[0] - LAYER - ROW
    low, high = rows_needed(run)
    main = (max(low, 0), min(high, voxels))
    rows = pl.ds(main[0], main[1] - main[0])
    to = pl.ds(main[0] - origin, main[1] - main[0])
    copies = [
        (nb_ref, nb),
        (f_ref.at[rows, :], xe.at[to, pl.ds(0, channels)]),
        (g_ref.at[rows, :], xe.at[to, pl.ds(channels, channels)]),
    ]
    if low < 0:
        copies.append(
            (halos.pop(0).at[pl.ds(LAYER + low, -low), :], xe.at[pl.ds(low - origin, -low), :])
        )
    if high > voxels:
        copies.append(
            (
                halos.pop(0).at[pl.ds(0, high - voxels), :],
                xe.at[pl.ds(voxels - origin, high - voxels), :],
            )
        )
    early = len(copies)
    copies.append((w_hbm, w_ref) if make_wt else (wt_hbm, wt))
    copies = [
        pltpu.make_async_copy(source, target, sems.at[i])
        for i, (source, target) in enumerate(copies)
    ]
    for copy in copies:
        copy.start()
    edge = jnp.zeros((ROW, 2 * channels), jnp.bfloat16)
    if low - origin:
        xe[0:ROW, :] = edge
    if high - origin < xe.shape[0]:
        xe[xe.shape[0] - ROW :, :] = edge
    copies[0].wait()
    for k in range(27):
        rel[k, :, :] = row_in_scene_window(nb[k], ROW * offset_of(k)[1])
    first_tile = run[0] // T
    for copy in copies[1:early]:
        copy.wait()

    spot = lax.broadcasted_iota(jnp.int32, (T, T), 0).astype(jnp.bfloat16)
    none = jnp.zeros((T, T), jnp.bfloat16)
    buffers = ((gf, gg), (gf2, gg2))

    def hot(tile, k):
        row = rel[k, first_tile + tile : first_tile + tile + 1, :]
        row = jnp.broadcast_to(row, (ROW, T)).astype(jnp.bfloat16)
        return one_hot(jnp.concatenate([row] * (T // ROW), axis=0) == spot)

    def gathers(chunk):
        to_f, to_g = buffers[chunk % 2]
        for h in range(CHUNK_C // T):
            tile = chunk * (CHUNK_C // T) + h
            cols = slice(h * T, (h + 1) * T)
            kept = []

            def put(k, part):
                to_f[k * T : (k + 1) * T, cols] = part[:channels]
                to_g[k * T : (k + 1) * T, cols] = part[channels:]

            def put_pair(source, right, pair):
                picked = jnp.dot(source, right, preferred_element_type=jnp.float32)
                picked = picked.astype(jnp.bfloat16)
                put(pair[0], picked[:, :T])
                put(pair[1], picked[:, T:])

            for dz in (-1, 0, 1):
                for dy in (-1, 0, 1):
                    start = tile * T + ROW + ROW * dy + LAYER * (dz + 1)
                    window = xe[start : start + T, :].T
                    first = 9 * (dz + 1) + 3 * (dy + 1)
                    pair = (first, first + 2)
                    right = jnp.concatenate([hot(tile, k) for k in pair], axis=1)
                    put_pair(window, right, pair)
                    if first + 1 == 13:
                        put(13, window)
                    else:
                        kept.append((first + 1, window))
                    if len(kept) == 2:
                        (k0, window0), (k1, window1) = kept
                        right = jnp.concatenate(
                            [
                                jnp.concatenate([hot(tile, k0), none], axis=1),
                                jnp.concatenate([none, hot(tile, k1)], axis=1),
                            ],
                            axis=0,
                        )
                        put_pair(jnp.concatenate([window0, window1], axis=1), right, (k0, k1))
                        kept = []
                    yield

    def product(chunk):
        rows = slice(chunk * CHUNK_C, (chunk + 1) * CHUNK_C)
        kernels = (slice(0, channels), slice(channels, 2 * channels))
        outs = ((conv_ref, conv_hbm), (gin_ref, gin_hbm))
        for (out, out_hbm), picked, side in zip(outs, buffers[chunk % 2], kernels):
            total = None
            for part in range(3):
                span = slice(part * 9 * T, (part + 1) * 9 * T)
                term = jnp.dot(wt[side, span], picked[span, :], preferred_element_type=jnp.float32)
                total = term if total is None else total + term
                if part == 2:
                    out[rows, :] = total.T.astype(jnp.bfloat16)
                    copy = pltpu.make_async_copy(
                        out.at[rows, :],
                        out_hbm.at[pl.ds(run[0] + chunk * CHUNK_C, CHUNK_C), :],
                        sems.at[len(copies) + len(written)],
                    )
                    copy.start()
                    written.append(copy)
                yield

    written = []
    pending = iter(())
    for chunk in range(size // CHUNK_C):
        for turn, _ in enumerate(gathers(chunk)):
            if turn % 3 == 2:
                next(pending, None)
        for _ in pending:
            pass
        if chunk == 0:
            for copy in copies[early:]:
                copy.wait()
            if make_wt:
                for k in range(27):
                    span = slice(k * T, (k + 1) * T)
                    wt[0:channels, span] = w_ref[span, :].T
                    wt[channels:, span] = w_ref[(26 - k) * T : (27 - k) * T, :]
        pending = product(chunk)
    for _ in pending:
        pass
    for copy in written:
        copy.wait()


def conv_run(feats, grads, low, high, neigh, weight, run, earlier, name):
    voxels, channels = feats.shape
    out = jax.ShapeDtypeStruct((voxels, channels), jnp.bfloat16)
    turned = jax.ShapeDtypeStruct((2 * channels, 27 * channels), jnp.bfloat16)
    make_wt = earlier is None
    operands = [feats, grads, neigh, weight]
    if not make_wt:
        conv_out, grad_in, wt = earlier
        operands += [wt, conv_out, grad_in]
    first, end = rows_needed(run)
    if first < 0:
        operands.append(low)
    if end > voxels:
        operands.append(high)
    hbm = pl.BlockSpec(memory_space=pltpu.HBM)
    size = run[1] - run[0]
    results = pl.pallas_call(
        functools.partial(conv_kernel, voxels, run, make_wt),
        out_shape=(out, out) + ((turned,) if make_wt else ()),
        in_specs=[hbm] * len(operands),
        out_specs=(hbm, hbm) + ((VMEM,) if make_wt else ()),
        input_output_aliases={} if make_wt else {5: 0, 6: 1},
        scratch_shapes=[
            pltpu.VMEM(weight.shape if make_wt else turned.shape, jnp.bfloat16),
            pltpu.VMEM((size, channels), jnp.bfloat16),
            pltpu.VMEM((size, channels), jnp.bfloat16),
            pltpu.VMEM((size + 2 * (LAYER + ROW), 2 * channels), jnp.bfloat16),
            pltpu.VMEM(neigh.shape, jnp.int32),
            pltpu.VMEM(neigh.shape, jnp.int32),
        ]
        + [pltpu.VMEM((27 * T, CHUNK_C), jnp.bfloat16)] * 4
        + [pltpu.SemaphoreType.DMA((8 + 2 * size // CHUNK_C,))],
        compiler_params=pltpu.CompilerParams(vmem_limit_bytes=CONV_VMEM_LIMIT),
        cost_estimate=pl.CostEstimate(flops=10**10, bytes_accessed=6 * 10**6, transcendentals=0),
        name=name,
    )(*operands)
    return tuple(results) if make_wt else (results[0], results[1], wt)


def sum_kernel(*refs):
    *parts, out_ref = refs
    terms = [ref[i] for ref in parts for i in range(ref.shape[0])]
    total = terms[0].astype(jnp.float32)
    for term in terms[1:]:
        total += term.astype(jnp.float32)
    total = total.astype(out_ref.dtype)
    for i in range(out_ref.shape[0]):
        out_ref[i] = total


def sum_parts(parts, copies, name):
    shape = parts[0].shape[1:]
    return pl.pallas_call(
        sum_kernel,
        out_shape=jax.ShapeDtypeStruct((copies,) + shape, parts[0].dtype),
        in_specs=[VMEM] * len(parts),
        out_specs=VMEM,
        compiler_params=pltpu.CompilerParams(vmem_limit_bytes=VMEM_LIMIT),
        name=name,
    )(*parts)


def widen_kernel(side_ref, in_ref, *rest):
    out_ref = rest[-1]
    out_ref[...] = in_ref[...].astype(out_ref.dtype)


def widen(rows, side, count, earlier, name):
    half, channels = rows.shape
    block = (half // 2, channels)
    return pl.pallas_call(
        widen_kernel,
        grid_spec=pltpu.PrefetchScalarGridSpec(
            num_scalar_prefetch=1,
            grid=(2,),
            in_specs=[pl.BlockSpec(block, lambda i, side: (i, 0))]
            + [pl.BlockSpec(memory_space=pl.ANY)] * len(earlier),
            out_specs=pl.BlockSpec(block, lambda i, side: (side[0] * 2 + i, 0)),
        ),
        out_shape=jax.ShapeDtypeStruct((count, channels), jnp.float32),
        input_output_aliases={2 + i: i for i in range(len(earlier))},
        compiler_params=pltpu.CompilerParams(vmem_limit_bytes=VMEM_LIMIT),
        name=name,
    )(side, rows, *earlier)


def local(features, neighbours, weight, grad_out):
    feats, grads = features[0], grad_out[0]
    voxels, channels = feats.shape
    neigh = neighbours.reshape(27, voxels // T, T)
    space, dp = lax.axis_size("space"), lax.axis_size("dp")
    up = [(i, i + 1) for i in range(space - 1)]
    down = [(i + 1, i) for i in range(space - 1)]
    last = jnp.concatenate([feats[voxels - LAYER :], grads[voxels - LAYER :]], axis=1)
    first = jnp.concatenate([feats[:LAYER], grads[:LAYER]], axis=1)
    low = lax.ppermute(last, "space", up)
    high = lax.ppermute(first, "space", down)

    scale = 1.0 / math.sqrt(dp * space * voxels)
    share = -(-27 * channels // (16 * dp)) * 16
    parity = (lax.axis_index("dp") % 2).astype(jnp.int32).reshape(1)
    inner = grad_w_inner(feats, grads, neigh)
    mine, other = grad_w_halo(feats, grads, low, neigh, inner, parity, scale, share * dp)
    swap = [(i, i ^ 1) for i in range(dp)]
    alike = [list(range(0, dp, 2)), list(range(1, dp, 2))]
    other = lax.ppermute(other, "dp", swap)
    mine = sum_parts((mine[None], other[None]), 1, "sum_of_pair")
    mine, flat_weight = lax.optimization_barrier(
        (mine, weight.reshape(27 * channels, channels))
    )
    chunks = voxels // CHUNK_C
    ends = [0, chunks // 4 * CHUNK_C, chunks * 2 // 3 * CHUNK_C, voxels]

    def conv(done, part):
        run = (ends[part], ends[part + 1])
        name = "conv_run_%d" % part
        return conv_run(feats, grads, low, high, neigh, flat_weight, run, done, name)

    def exchange(pieces):
        return lax.all_to_all(pieces, "dp", 0, 0, axis_index_groups=alike, tiled=True)

    pieces = exchange(mine.reshape(dp // 2, share, channels))
    done = conv(None, 0)
    pieces, done, high = lax.optimization_barrier((pieces, done, high))
    pieces = lax.all_to_all(sum_parts((pieces,), space, "sum_for_space"), "space", 0, 0, tiled=True)
    done = conv(done, 1)
    pieces, done = lax.optimization_barrier((pieces, done))
    pieces = exchange(sum_parts((pieces,), dp // 2, "sum_for_dp"))
    done = conv(done, 2)
    pieces, done = lax.optimization_barrier((pieces, done))
    mine = pieces.reshape(dp // 2 * share, channels)
    other = lax.ppermute(mine, "dp", swap)
    grad_w = widen(mine, parity, 27 * channels, (), "widen_own_half")
    grad_w = widen(other, 1 - parity, 27 * channels, (grad_w,), "widen_other_half")
    conv_out, grad_in, _ = done
    return conv_out[None], grad_in[None], grad_w.reshape(27, channels, channels)


def solution(mesh):
    in_specs = (P("dp", "space", None), P("dp", None, "space"), P(), P("dp", "space", None))
    out_specs = (P("dp", "space", None), P("dp", "space", None), P())
    return jax.shard_map(local, mesh=mesh, in_specs=in_specs, out_specs=out_specs, check_vma=False)
```

profile of v0, /device:TPU:0, one launch (start us, length us, event | category | flops | bytes accessed | tf_op | source)
XLA Modules:
  0.0 73.7 jit_solution(15278287736076460172)
XLA Ops:
  0.6 0.0 copy-start
  0.6 0.0 copy-start.1
  0.7 0.0 copy-start.3
  0.7 1.4 %slice_bitcast_fusion = (bf16[1024,128]{1,0:T(8,128)(2,1)S(1)}, bf16[1024,128]{1,0:T(8,128)(2,1)S(1)}, bf16[1024,128]{1,0:T(8,128)(2,1)S(1)}, bf16[1024,128]{1,0:T(8,128)(2,1)S(1)}) fusion(bf16[1,3072,128]{2,1,0:T(8,128)(2,1)} %param.7, bf16[1,3072,128]{2,1,0:T(8,128)(2,1)} %param.4), kind=kLoop, calls=%fused_computation.2 | loop fusion | bytes 2097152 | tf_op jit(solution)/shard_map/slice | solution.py:412
  2.1 0.9 %pad_maximum_fusion = bf16[1024,256]{1,0:T(8,128)(2,1)} fusion(bf16[1024,128]{1,0:T(8,128)(2,1)S(1)} %get-tuple-element.52, bf16[1024,128]{1,0:T(8,128)(2,1)S(1)} %get-tuple-element.53), kind=kLoop, calls=%fused_computation | loop fusion | flops 1048576 | bytes 1048576 | tf_op jit(solution)/shard_map/concatenate | solution.py:411
  2.9 4.9 %collective-permute-start = (bf16[1024,256]{1,0:T(8,128)(2,1)}, bf16[1024,256]{1,0:T(8,128)(2,1)S(1)}, u32[]{:S(2)}, u32[]{:S(2)}) collective-permute-start(bf16[1024,256]{1,0:T(8,128)(2,1)} %pad_maximum_fusion), channel_id=1, source_target_pairs={{0,1},{1,2},{2,3},{4,5},{5,6},{6,7},{8,9},{9,10},{10,11},{12,13},{... | collective-permute-start | bytes 1572872 | tf_op jit(solution)/shard_map/ppermute | solution.py:413
  7.9 0.0 copy-done
  7.9 0.0 copy-done.1
  7.9 0.0 copy-done.3
  7.9 9.9 %weight_gradient_inner.1.in_ref = f32[128,3456]{1,0:T(8,128)S(1)} custom-call(bf16[3072,128]{1,0:T(8,128)(2,1)S(1)} %bitcast.27, bf16[3072,128]{1,0:T(8,128)(2,1)S(1)} %bitcast.32, s32[27,24,128]{2,1,0:T(8,128)S(1)} %bitcast.37), custom_call_target="tpu_custom_call" | custom-call | flops 8000000000 | bytes 4000000 | tf_op jit(solution)/shard_map/weight_gradient_inner/pallas_call | solution.py:132
  17.9 1.5 %collective-permute-done.low_ref.rest_0_.rest_3_ = bf16[1024,256]{1,0:T(8,128)(2,1)S(1)} collective-permute-done((bf16[1024,256]{1,0:T(8,128)(2,1)}, bf16[1024,256]{1,0:T(8,128)(2,1)S(1)}, u32[]{:S(2)}, u32[]{:S(2)}) %collective-permute-start) | collective-permute-done | bytes 524320 | tf_op jit(solution)/shard_map/ppermute | solution.py:413
  19.3 0.0 copy-start.2
  19.3 3.6 %weight_gradient_halo.1 = (bf16[1728,128]{1,0:T(8,128)(2,1)S(1)}, bf16[1728,128]{1,0:T(8,128)(2,1)S(1)}) custom-call(s32[1]{0:T(128)} %bitcast.parity_ref.side_ref, bf16[3072,128]{1,0:T(8,128)(2,1)S(1)} %bitcast.28, bf16[3072,128]{1,0:T(8,128)(2,1)S(1)} %bitcast.33, bf16[1024,256]{1,0:T(8,128)(2,1)S(1)} %collective-permute-done.low_ref.rest_0_.rest_3_, ...), custom_call_target="tpu_custom_call" | custom-call | flops 3000000000 | bytes 4000000 | tf_op jit(solution)/shard_map/weight_gradient_halo/pallas_call | solution.py:147
  23.0 0.0 copy-done.2
  23.0 0.1 collective-permute-start.1
  23.0 0.1 pad_maximum_fusion.1
  23.1 1.3 %collective-permute-start.2 = (bf16[1024,256]{1,0:T(8,128)(2,1)S(1)}, bf16[1024,256]{1,0:T(8,128)(2,1)S(1)}, u32[]{:S(2)}, u32[]{:S(2)}) collective-permute-start(bf16[1024,256]{1,0:T(8,128)(2,1)S(1)} %pad_maximum_fusion.1), channel_id=1, source_target_pairs={{1,0},{2,1},{3,2},{5,4},{6,5},{7,6},{9,8},{10,9},{11,10},{13,12},{... | collective-permute-start | bytes 1572872 | tf_op jit(solution)/shard_map/ppermute | solution.py:414
  24.4 0.4 collective-permute-done.1
  24.8 0.9 %sum_of_pair.1 = bf16[1,1728,128]{2,1,0:T(8,128)(2,1)} custom-call(bf16[1,1728,128]{2,1,0:T(8,128)(2,1)S(1)} %bitcast.22, bf16[1,1728,128]{2,1,0:T(8,128)(2,1)S(1)} %bitcast.23), custom_call_target="tpu_custom_call" | custom-call | tf_op jit(solution)/shard_map/sum_of_pair/pallas_call | solution.py:370
  25.7 3.7 %all-to-all-start = ((bf16[4,432,128]{2,1,0:T(8,128)(2,1)}), bf16[4,432,128]{2,1,0:T(8,128)(2,1)S(1)}, u32[]{:S(2)}, u32[]{:S(2)}) async-start(bf16[4,432,128]{2,1,0:T(8,128)(2,1)} %bitcast.9), calls=%async_computation | async-start | bytes 884736 | tf_op jit(solution)/shard_map/all_to_all | solution.py:437
  29.5 8.2 %conv_run_0.1 = (bf16[3072,128]{1,0:T(8,128)(2,1)}, bf16[3072,128]{1,0:T(8,128)(2,1)}, bf16[256,3456]{1,0:T(8,128)(2,1)}) custom-call(bf16[3072,128]{1,0:T(8,128)(2,1)} %bitcast.24, bf16[3072,128]{1,0:T(8,128)(2,1)} %bitcast.29, s32[27,24,128]{2,1,0:T(8,128)} %bitcast.34, bf16[3456,128]{1,0:T(8,128)(2,1)} %bitcast.40, bf16[1024,256]{1,0:T(8,128)(2,1)} %copy-done.2), custom_call_target="tpu_custom_call" | custom-call | flops 10000000000 | bytes 6000000 | tf_op jit(solution)/shard_map/conv_run_0/pallas_call | solution.py:334
  37.6 2.3 %collective-permute-done.2.rest_3_ = bf16[1024,256]{1,0:T(8,128)(2,1)S(1)} collective-permute-done((bf16[1024,256]{1,0:T(8,128)(2,1)S(1)}, bf16[1024,256]{1,0:T(8,128)(2,1)S(1)}, u32[]{:S(2)}, u32[]{:S(2)}) %collective-permute-start.2) | collective-permute-done | bytes 524320 | tf_op jit(solution)/shard_map/ppermute | solution.py:414
  40.0 0.0 copy-start.4
  40.0 0.0 all-to-all-done.refs_0_
  40.0 0.9 %sum_for_space.1 = bf16[4,432,128]{2,1,0:T(8,128)(2,1)} custom-call(bf16[4,432,128]{2,1,0:T(8,128)(2,1)S(1)} %all-to-all-done.refs_0_), custom_call_target="tpu_custom_call" | custom-call | tf_op jit(solution)/shard_map/sum_for_space/pallas_call | solution.py:370
  40.9 4.0 %all-to-all-start.1 = ((bf16[4,432,128]{2,1,0:T(8,128)(2,1)}), bf16[4,432,128]{2,1,0:T(8,128)(2,1)S(1)}, u32[]{:S(2)}, u32[]{:S(2)}) async-start(bf16[4,432,128]{2,1,0:T(8,128)(2,1)} %sum_for_space.1), calls=%async_computation.1 | async-start | bytes 884736 | tf_op jit(solution)/shard_map/all_to_all | solution.py:442
  44.9 9.8 %conv_run_1.1 = (bf16[3072,128]{1,0:T(8,128)(2,1)}, bf16[3072,128]{1,0:T(8,128)(2,1)}) custom-call(bf16[3072,128]{1,0:T(8,128)(2,1)} %bitcast.25, bf16[3072,128]{1,0:T(8,128)(2,1)} %bitcast.30, s32[27,24,128]{2,1,0:T(8,128)} %bitcast.35, bf16[3456,128]{1,0:T(8,128)(2,1)} %bitcast.41, ...), custom_call_target="tpu_custom_call", output_to_operand_aliasing={{0}: (5, {}), {1}: (6, {})} | custom-call | flops 10000000000 | bytes 6000000 | tf_op jit(solution)/shard_map/conv_run_1/pallas_call | solution.py:334
  54.8 0.0 copy-done.4
  54.8 3.0 %all-to-all-done.1.refs_0_ = bf16[4,432,128]{2,1,0:T(8,128)(2,1)S(1)} async-done(((bf16[4,432,128]{2,1,0:T(8,128)(2,1)}), bf16[4,432,128]{2,1,0:T(8,128)(2,1)S(1)}, u32[]{:S(2)}, u32[]{:S(2)}) %all-to-all-start.1) | async-done | bytes 442400 | tf_op jit(solution)/shard_map/all_to_all | solution.py:442
  57.8 0.8 %sum_for_dp.1 = bf16[4,432,128]{2,1,0:T(8,128)(2,1)} custom-call(bf16[4,432,128]{2,1,0:T(8,128)(2,1)S(1)} %all-to-all-done.1.refs_0_), custom_call_target="tpu_custom_call" | custom-call | tf_op jit(solution)/shard_map/sum_for_dp/pallas_call | solution.py:370
  58.6 3.9 %all-to-all-start.2 = ((bf16[4,432,128]{2,1,0:T(8,128)(2,1)}), bf16[4,432,128]{2,1,0:T(8,128)(2,1)S(1)}, u32[]{:S(2)}, u32[]{:S(2)}) async-start(bf16[4,432,128]{2,1,0:T(8,128)(2,1)} %sum_for_dp.1), calls=%async_computation.2 | async-start | bytes 884736 | tf_op jit(solution)/shard_map/all_to_all | solution.py:437
  62.5 8.4 %conv_run_2.1 = (bf16[3072,128]{1,0:T(8,128)(2,1)}, bf16[3072,128]{1,0:T(8,128)(2,1)}) custom-call(bf16[3072,128]{1,0:T(8,128)(2,1)} %bitcast.26, bf16[3072,128]{1,0:T(8,128)(2,1)} %bitcast.31, s32[27,24,128]{2,1,0:T(8,128)} %bitcast.36, bf16[3456,128]{1,0:T(8,128)(2,1)} %bitcast.42, ...), custom_call_target="tpu_custom_call", output_to_operand_aliasing={{0}: (5, {}), {1}: (6, {})} | custom-call | flops 10000000000 | bytes 6000000 | tf_op jit(solution)/shard_map/conv_run_2/pallas_call | solution.py:334
  70.9 0.0 all-to-all-done.2
  70.9 0.1 collective-permute-start.3
  71.0 1.0 %widen_own_half.1.rest_0_ = f32[3456,128]{1,0:T(8,128)} custom-call(s32[1]{0:T(128)} %bitcast.parity_ref.side_ref, bf16[1728,128]{1,0:T(8,128)(2,1)S(1)} %bitcast.21), custom_call_target="tpu_custom_call" | custom-call | tf_op jit(solution)/shard_map/widen_own_half/pallas_call | solution.py:388
  72.0 0.8 %collective-permute-done.3.in_ref = bf16[1728,128]{1,0:T(8,128)(2,1)S(1)} collective-permute-done((bf16[1728,128]{1,0:T(8,128)(2,1)S(1)}, bf16[1728,128]{1,0:T(8,128)(2,1)S(1)}, u32[]{:S(2)}, u32[]{:S(2)}) %collective-permute-start.3) | collective-permute-done | bytes 442400 | tf_op jit(solution)/shard_map/ppermute | solution.py:449
  72.8 0.9 %widen_other_half.1 = f32[3456,128]{1,0:T(8,128)} custom-call(s32[1]{0:T(128)S(6)} %sub.3.side_ref, bf16[1728,128]{1,0:T(8,128)(2,1)S(1)} %collective-permute-done.3.in_ref, f32[3456,128]{1,0:T(8,128)} %widen_own_half.1.rest_0_), custom_call_target="tpu_custom_call", output_to_operand_aliasing={{}: (2, {})} | custom-call | tf_op jit(solution)/shard_map/widen_other_half/pallas_call | solution.py:388
Async XLA Ops:
  0.6 7.3 %copy-start = (bf16[1,3072,128]{2,1,0:T(8,128)(2,1)S(1)}, bf16[1,3072,128]{2,1,0:T(8,128)(2,1)}, u32[]{:S(2)}) copy-start(bf16[1,3072,128]{2,1,0:T(8,128)(2,1)} %param.4) | copy-start | bytes 2359300
  0.6 7.2 %copy-start.1 = (bf16[1,3072,128]{2,1,0:T(8,128)(2,1)S(1)}, bf16[1,3072,128]{2,1,0:T(8,128)(2,1)}, u32[]{:S(2)}) copy-start(bf16[1,3072,128]{2,1,0:T(8,128)(2,1)} %param.7) | copy-start | bytes 2359300
  0.7 7.2 %copy-start.3 = (s32[1,27,3072]{2,0,1:T(1,128)S(1)}, s32[1,27,3072]{2,0,1:T(1,128)}, u32[]{:S(2)}) copy-start(s32[1,27,3072]{2,0,1:T(1,128)} %param.5) | copy-start | bytes 995332
  2.9 16.4 %collective-permute-start = (bf16[1024,256]{1,0:T(8,128)(2,1)}, bf16[1024,256]{1,0:T(8,128)(2,1)S(1)}, u32[]{:S(2)}, u32[]{:S(2)}) collective-permute-start(bf16[1024,256]{1,0:T(8,128)(2,1)} %pad_maximum_fusion), channel_id=1, source_target_pairs={{0,1},{1,2},{2,3},{4,5},{5,6},{6,7},{8,9},{9,10},{10,11},{12,13},{... | collective-permute-start | bytes 1572872 | tf_op jit(solution)/shard_map/ppermute | solution.py:413
  19.3 3.6 %copy-start.2 = (bf16[1024,256]{1,0:T(8,128)(2,1)}, bf16[1024,256]{1,0:T(8,128)(2,1)S(1)}, u32[]{:S(2)}) copy-start(bf16[1024,256]{1,0:T(8,128)(2,1)S(1)} %collective-permute-done.low_ref.rest_0_.rest_3_) | copy-start | bytes 1572868
  23.0 1.9 %collective-permute-start.1 = (bf16[1728,128]{1,0:T(8,128)(2,1)S(1)}, bf16[1728,128]{1,0:T(8,128)(2,1)S(1)}, u32[]{:S(2)}, u32[]{:S(2)}) collective-permute-start(bf16[1728,128]{1,0:T(8,128)(2,1)S(1)} %get-tuple-element.27), channel_id=1, source_target_pairs={{0,4},{4,0},{8,12},{12,8},{16,20},{20,16},{24,28},{28,24},{1,5},{5... | collective-permute-start | bytes 1327112 | tf_op jit(solution)/shard_map/ppermute | solution.py:423
  23.1 16.9 %collective-permute-start.2 = (bf16[1024,256]{1,0:T(8,128)(2,1)S(1)}, bf16[1024,256]{1,0:T(8,128)(2,1)S(1)}, u32[]{:S(2)}, u32[]{:S(2)}) collective-permute-start(bf16[1024,256]{1,0:T(8,128)(2,1)S(1)} %pad_maximum_fusion.1), channel_id=1, source_target_pairs={{1,0},{2,1},{3,2},{5,4},{6,5},{7,6},{9,8},{10,9},{11,10},{13,12},{... | collective-permute-start | bytes 1572872 | tf_op jit(solution)/shard_map/ppermute | solution.py:414
  25.7 14.2 %all-to-all-start = ((bf16[4,432,128]{2,1,0:T(8,128)(2,1)}), bf16[4,432,128]{2,1,0:T(8,128)(2,1)S(1)}, u32[]{:S(2)}, u32[]{:S(2)}) async-start(bf16[4,432,128]{2,1,0:T(8,128)(2,1)} %bitcast.9), calls=%async_computation | async-start | bytes 884736 | tf_op jit(solution)/shard_map/all_to_all | solution.py:437
  40.0 14.8 %copy-start.4 = (bf16[1024,256]{1,0:T(8,128)(2,1)}, bf16[1024,256]{1,0:T(8,128)(2,1)S(1)}, u32[]{:S(2)}) copy-start(bf16[1024,256]{1,0:T(8,128)(2,1)S(1)} %collective-permute-done.2.rest_3_) | copy-start | bytes 1572868
  40.9 16.9 %all-to-all-start.1 = ((bf16[4,432,128]{2,1,0:T(8,128)(2,1)}), bf16[4,432,128]{2,1,0:T(8,128)(2,1)S(1)}, u32[]{:S(2)}, u32[]{:S(2)}) async-start(bf16[4,432,128]{2,1,0:T(8,128)(2,1)} %sum_for_space.1), calls=%async_computation.1 | async-start | bytes 884736 | tf_op jit(solution)/shard_map/all_to_all | solution.py:442
  58.6 12.3 %all-to-all-start.2 = ((bf16[4,432,128]{2,1,0:T(8,128)(2,1)}), bf16[4,432,128]{2,1,0:T(8,128)(2,1)S(1)}, u32[]{:S(2)}, u32[]{:S(2)}) async-start(bf16[4,432,128]{2,1,0:T(8,128)(2,1)} %sum_for_dp.1), calls=%async_computation.2 | async-start | bytes 884736 | tf_op jit(solution)/shard_map/all_to_all | solution.py:437
  70.9 1.9 %collective-permute-start.3 = (bf16[1728,128]{1,0:T(8,128)(2,1)S(1)}, bf16[1728,128]{1,0:T(8,128)(2,1)S(1)}, u32[]{:S(2)}, u32[]{:S(2)}) collective-permute-start(bf16[1728,128]{1,0:T(8,128)(2,1)S(1)} %bitcast.20), channel_id=1, source_target_pairs={{0,4},{4,0},{8,12},{12,8},{16,20},{20,16},{24,28},{28,24},{1,5},{5... | collective-permute-start | bytes 1327112 | tf_op jit(solution)/shard_map/ppermute | solution.py:449
where the time goes:
time: 74.1 us; the launch traced here: 73.7 us
  Pallas kernels  44.5 us (60%)
  starting transfers between devices  18 us (24%)
  waiting for transfers between devices  8.04 us (11%)
  local copies, waits for them, and re-layouts  1.42 us (2%)
  other arithmetic  0.91 us (1%)
  between operations  0.8 us (1%)
    pallas_call x3, Pallas kernels, conv_run(): pl.pallas_call(functools.partial(conv_kernel, voxels, run, make_wt), out_...  26.4 us
    pallas_call x1, Pallas kernels, grad_w_inner(): pl.pallas_call(functools.partial(weight_inner_kernel, voxels), out_shape=...  9.94 us
    all_to_all x2, starting transfers between devices, exchange(): lax.all_to_all(pieces, 'dp', 0, 0, axis_index_groups=alike, tiled=True)  7.59 us
    ppermute x1, starting transfers between devices, local(): low = lax.ppermute(last, 'space', up)  4.95 us
    all_to_all x1, starting transfers between devices, local(): lax.all_to_all(sum_parts((pieces,), space, 'sum_for_space'), 'space', 0,...  4.04 us
    pallas_call x1, Pallas kernels, grad_w_halo(): pl.pallas_call(functools.partial(weight_halo_kernel, scale), out_shape=(o...  3.63 us
    all_to_all x1, waiting for transfers between devices, local(): lax.all_to_all(sum_parts((pieces,), space, 'sum_for_space'), 'space', 0,...  3.01 us
    pallas_call x3, Pallas kernels, sum_parts(): pl.pallas_call(sum_kernel, out_shape=jax.ShapeDtypeStruct((copies,) + sha...  2.66 us
  transfers between devices with their start and end apart: 7, of which 5 were waited for; matrix products, arithmetic and copies ran while one was open for 0% of the time, Pallas kernels for 52%

commit v1 on v0

--- a/solution.py
+++ b/solution.py
@@ -12,12 +12,13 @@
 ROW = PSIDE // 4
 LAYER = PSIDE * ROW
 T = 128
-CHUNK_W = 512
+CHUNK_W = 256
 CHUNK_C = 256
 VMEM_LIMIT = 28 * 1024 * 1024
-CONV_VMEM_LIMIT = 58 * 1024 * 1024
+FULL_VMEM_LIMIT = 58 * 1024 * 1024
 VMEM = pl.BlockSpec(memory_space=pltpu.VMEM)
 SMEM = pl.BlockSpec(memory_space=pltpu.SMEM)
+HBM = pl.BlockSpec(memory_space=pltpu.HBM)
 
 
 def offset_of(k):
@@ -48,68 +49,111 @@
             shift[k : k + 1, :] = jnp.full((1, T), ROW * offset_of(k)[1], jnp.int32)
 
 
-def add_weight_terms(o, ks, source, center, f_ref, g_ref, nb_ref, xe, shift, gf, gg, acc):
+def weight_terms(chunks, ks_of, source, f_ref, g_ref, nb_ref, xe, shift, buffers, acc, aside):
     channels = f_ref.shape[1]
     spot = lax.broadcasted_iota(jnp.int32, (T, T), 1).astype(jnp.bfloat16)
-    base = pl.multiple_of(o * CHUNK_W, CHUNK_W)
     pads = jnp.full((5, T), -1, jnp.int32)
-    for h in range(CHUNK_W // T):
-        rows = slice(h * T, (h + 1) * T)
-        mine = jnp.concatenate([nb_ref[:, o * (CHUNK_W // T) + h, :], pads], axis=0)
-        mine = row_in_scene_window(mine, shift[...]).T.astype(jnp.bfloat16)
-        for dz, dy in sorted({offset_of(k)[:2] for k in ks}):
-            some = [k for k in ks if offset_of(k)[:2] == (dz, dy)]
-            start = base + (source + h * T + ROW * dy + LAYER * dz)
-            window = xe[pl.ds(pl.multiple_of(start, ROW), T), :]
-            hot = jnp.concatenate([one_hot(mine[:, k : k + 1] == spot) for k in some], axis=0)
-            picked = jnp.dot(hot, window, preferred_element_type=jnp.float32)
-            picked = picked.astype(jnp.bfloat16)
-            for q, k in enumerate(some):
-                part = picked[q * T : (q + 1) * T]
-                gf[rows, k * T : (k + 1) * T] = part[:, :channels]
-                gg[rows, k * T : (k + 1) * T] = part[:, channels:]
-    here = pl.ds(base, CHUNK_W)
-    if center:
-        gg[:, 13 * T :] = g_ref[here, :]
-    span = slice(ks[0] * T, (ks[-1] + 1) * T)
-    acc[:, span] += jnp.dot(g_ref[here, :].T, gf[:, span], preferred_element_type=jnp.float32)
-    last = ks[-1] + 1 + (1 if center else 0)
-    span = slice(ks[0] * T, last * T)
-    to = slice((13 + ks[0]) * T, (13 + last) * T)
-    acc[:, to] += jnp.dot(f_ref[here, :].T, gg[:, span], preferred_element_type=jnp.float32)
-
-
-def weight_inner_kernel(voxels, f_ref, g_ref, nb_ref, acc, xe, shift, gf, gg):
+
+    def gathers(chunk):
+        to_f, to_g = buffers[chunk % 2]
+        ks = ks_of(chunk)
+        for h in range(CHUNK_W // T):
+            tile = chunk * (CHUNK_W // T) + h
+            rows = slice(h * T, (h + 1) * T)
+            mine = jnp.concatenate([nb_ref[:, tile, :], pads], axis=0)
+            mine = row_in_scene_window(mine, shift[...]).T.astype(jnp.bfloat16)
+            for dz, dy in sorted({offset_of(k)[:2] for k in ks if k < 13}):
+                some = [k for k in ks if k < 13 and offset_of(k)[:2] == (dz, dy)]
+                start = tile * T + source + ROW * dy + LAYER * dz
+                window = xe[start : start + T, :]
+                hot = jnp.concatenate([one_hot(mine[:, k : k + 1] == spot) for k in some], axis=0)
+                picked = jnp.dot(hot, window, preferred_element_type=jnp.float32)
+                picked = picked.astype(jnp.bfloat16)
+                for q, k in enumerate(some):
+                    part = picked[q * T : (q + 1) * T]
+                    to_f[rows, k * T : (k + 1) * T] = part[:, :channels]
+                    to_g[rows, k * T : (k + 1) * T] = part[:, channels:]
+                yield
+
+    def product(chunk):
+        here = slice(chunk * CHUNK_W, (chunk + 1) * CHUNK_W)
+        picked_f, picked_g = buffers[chunk % 2]
+        ks = ks_of(chunk)
+        if 13 in ks:
+            picked_g[:, 13 * T :] = g_ref[here, :]
+        for ref, picked, side, end in ((g_ref, picked_f, 0, 13), (f_ref, picked_g, 13, 14)):
+            left = ref[here, :].T
+            for group in (range(0, 4), range(4, 8), range(8, end)):
+                group = [k for k in group if k in ks]
+                if group:
+                    span = slice(group[0] * T, (group[-1] + 1) * T)
+                    to = slice((side + group[0]) * T, (side + group[-1] + 1) * T)
+                    acc[:, to] += jnp.dot(left, picked[:, span], preferred_element_type=jnp.float32)
+                    yield
+
+    pending = iter(())
+    for chunk in chunks:
+        for turn, _ in enumerate(gathers(chunk)):
+            next(pending, None)
+            if turn % 2:
+                next(aside, None)
+        for _ in pending:
+            pass
+        pending = product(chunk)
+    for _ in pending:
+        pass
+    for _ in aside:
+        pass
+
+
+def weight_inner_kernel(voxels, f_ref, g_ref, nb_ref, w_hbm, acc, wt_hbm, xe, shift, w_ref, wt, gf, gg, gf2, gg2, sems):
+    channels = f_ref.shape[1]
+    fetch = pltpu.make_async_copy(w_hbm, w_ref, sems.at[0])
+    fetch.start()
     beside(xe, ROW, f_ref, g_ref, voxels)
     fill_edges(xe, shift)
     acc[...] = jnp.zeros_like(acc)
-    rest = (f_ref, g_ref, nb_ref, xe, shift, gf, gg, acc)
-
-    @pl.loop(0, LAYER // CHUNK_W)
-    def _(o):
-        add_weight_terms(o, list(range(9, 13)), ROW, True, *rest)
-
-    @pl.loop(LAYER // CHUNK_W, voxels // CHUNK_W)
-    def _(o):
-        add_weight_terms(o, list(range(13)), ROW, True, *rest)
-
-
-def weight_halo_kernel(scale, parity_ref, f_ref, g_ref, low_ref, nb_ref, in_ref, mine_ref, other_ref, xe, shift, gf, gg, acc, out_ref):
-    xe[ROW : ROW + LAYER, :] = low_ref[...]
+    store = pltpu.make_async_copy(wt, wt_hbm, sems.at[1])
+
+    def turn_weights():
+        fetch.wait()
+        for k in range(27):
+            span = slice(k * T, (k + 1) * T)
+            wt[0:channels, span] = w_ref[span, :].T
+            wt[channels:, span] = w_ref[(26 - k) * T : (27 - k) * T, :]
+            if k % 2:
+                yield
+        store.start()
+
+    def ks_of(chunk):
+        return range(9 if chunk < LAYER // CHUNK_W else 0, 14)
+
+    chunks = range(voxels // CHUNK_W)
+    buffers = ((gf, gg), (gf2, gg2))
+    weight_terms(chunks, ks_of, ROW, f_ref, g_ref, nb_ref, xe, shift, buffers, acc, turn_weights())
+    store.wait()
+
+
+def weight_halo_kernel(scale, parity_ref, f_ref, g_ref, low_ref, nb_ref, in_ref, mine_ref, other_ref, xe, shift, gf, gg, gf2, gg2, acc, out_ref):
+    channels = f_ref.shape[1]
+    xe[ROW : ROW + LAYER, 0:channels] = low_ref[0]
+    xe[ROW : ROW + LAYER, channels:] = low_ref[1]
     fill_edges(xe, shift)
-    acc[...] = in_ref[...]
-    rest = (f_ref, g_ref, nb_ref, xe, shift, gf, gg, acc)
-
-    @pl.loop(0, LAYER // CHUNK_W)
-    def _(o):
-        add_weight_terms(o, list(range(9)), ROW + LAYER, False, *rest)
+    acc[...] = jnp.zeros_like(acc)
+    chunks = range(LAYER // CHUNK_W)
+    buffers = ((gf, gg), (gf2, gg2))
+    weight_terms(
+        chunks, lambda _: range(9), ROW + LAYER, f_ref, g_ref, nb_ref, xe, shift, buffers, acc, iter(())
+    )
+
+    def total(block, touched):
+        span = slice(block * T, (block + 1) * T)
+        return (in_ref[:, span] + acc[:, span] if touched else in_ref[:, span]) * scale
 
     for k in range(13):
-        out_ref[k * T : (k + 1) * T, :] = (acc[:, k * T : (k + 1) * T].T * scale).astype(out_ref.dtype)
+        out_ref[k * T : (k + 1) * T, :] = total(k, k < 9).T.astype(out_ref.dtype)
     for k in range(14):
-        out_ref[(26 - k) * T : (27 - k) * T, :] = (
-            acc[:, (13 + k) * T : (14 + k) * T] * scale
-        ).astype(out_ref.dtype)
+        out_ref[(26 - k) * T : (27 - k) * T, :] = total(13 + k, k < 9).astype(out_ref.dtype)
     if out_ref.shape[0] > 27 * T:
         out_ref[27 * T :, :] = jnp.zeros((out_ref.shape[0] - 27 * T, out_ref.shape[1]), out_ref.dtype)
     half = out_ref.shape[0] // 2
@@ -118,27 +162,39 @@
     other_ref[...] = out_ref[pl.ds(pl.multiple_of((1 - parity) * half, 16), half), :]
 
 
-def weight_scratch(rows, channels):
+def rows_scratch(rows, channels):
     return [
         pltpu.VMEM((rows + 2 * ROW, 2 * channels), jnp.bfloat16),
         pltpu.VMEM((32, T), jnp.int32),
+    ]
+
+
+def gathered_scratch():
+    return [
         pltpu.VMEM((CHUNK_W, 13 * T), jnp.bfloat16),
         pltpu.VMEM((CHUNK_W, 14 * T), jnp.bfloat16),
-    ]
-
-
-def grad_w_inner(feats, grads, neigh):
+    ] * 2
+
+
+def grad_w_inner(feats, grads, neigh, weight):
     voxels, channels = feats.shape
+    turned = (2 * channels, 27 * channels)
     return pl.pallas_call(
         functools.partial(weight_inner_kernel, voxels),
-        out_shape=jax.ShapeDtypeStruct((channels, 27 * T), jnp.float32),
-        in_specs=[VMEM] * 3,
-        out_specs=VMEM,
-        scratch_shapes=weight_scratch(voxels, channels),
+        out_shape=(
+            jax.ShapeDtypeStruct((channels, 27 * T), jnp.float32),
+            jax.ShapeDtypeStruct(turned, jnp.bfloat16),
+        ),
+        in_specs=[VMEM] * 3 + [HBM],
+        out_specs=(VMEM, HBM),
+        scratch_shapes=rows_scratch(voxels, channels)
+        + [pltpu.VMEM(weight.shape, jnp.bfloat16), pltpu.VMEM(turned, jnp.bfloat16)]
+        + gathered_scratch()
+        + [pltpu.SemaphoreType.DMA((2,))],
         compiler_params=pltpu.CompilerParams(vmem_limit_bytes=VMEM_LIMIT),
         cost_estimate=pl.CostEstimate(flops=8 * 10**9, bytes_accessed=4 * 10**6, transcendentals=0),
         name="weight_gradient_inner",
-    )(feats, grads, neigh)
+    )(feats, grads, neigh, weight)
 
 
 def grad_w_halo(feats, grads, low, neigh, partial, parity, scale, rows):
@@ -149,7 +205,8 @@
         out_shape=(out, out),
         in_specs=[SMEM] + [VMEM] * 5,
         out_specs=(VMEM, VMEM),
-        scratch_shapes=weight_scratch(LAYER, channels)
+        scratch_shapes=rows_scratch(LAYER, channels)
+        + gathered_scratch()
         + [
             pltpu.VMEM((channels, 27 * T), jnp.float32),
             pltpu.VMEM((rows, channels), jnp.bfloat16),
@@ -160,6 +217,29 @@
     )(parity, feats, grads, low, neigh, partial)
 
 
+def stack_kernel(f_last, g_last, f_first, g_first, last, first):
+    last[0] = f_last[...]
+    last[1] = g_last[...]
+    first[0] = f_first[...]
+    first[1] = g_first[...]
+
+
+def stack_edges(feats, grads):
+    voxels, channels = feats.shape
+    out = jax.ShapeDtypeStruct((2, LAYER, channels), jnp.bfloat16)
+    end = pl.BlockSpec((LAYER, channels), lambda i: (voxels // LAYER - 1, 0))
+    start = pl.BlockSpec((LAYER, channels), lambda i: (0, 0))
+    return pl.pallas_call(
+        stack_kernel,
+        grid=(1,),
+        out_shape=(out, out),
+        in_specs=[end, end, start, start],
+        out_specs=(VMEM, VMEM),
+        compiler_params=pltpu.CompilerParams(vmem_limit_bytes=FULL_VMEM_LIMIT),
+        name="stack_edges",
+    )(feats, grads, feats, grads)
+
+
 def rows_needed(run):
     first, end = run
     return (
@@ -168,14 +248,9 @@
     )
 
 
-def conv_kernel(voxels, run, make_wt, f_ref, g_ref, nb_ref, w_hbm, *rest):
-    if make_wt:
-        conv_hbm, gin_hbm, wt, w_ref, *scratch = rest[-14:]
-    else:
-        wt_hbm = rest[0]
-        conv_hbm, gin_hbm, wt, *scratch = rest[-13:]
-    conv_ref, gin_ref, xe, nb, rel, gf, gg, gf2, gg2, sems = scratch
-    halos = list(rest[(0 if make_wt else 3) :])
+def conv_kernel(voxels, run, halos, f_ref, g_ref, nb_ref, wt_hbm, *rest):
+    halos = list(rest[:halos])
+    conv_hbm, gin_hbm, wt, conv_ref, gin_ref, xe, nb, rel, gf, gg, gf2, gg2, sems = rest[-13:]
     channels = f_ref.shape[1]
     size = run[1] - run[0]
 
@@ -189,19 +264,17 @@
         (f_ref.at[rows, :], xe.at[to, pl.ds(0, channels)]),
         (g_ref.at[rows, :], xe.at[to, pl.ds(channels, channels)]),
     ]
+    parts = []
     if low < 0:
-        copies.append(
-            (halos.pop(0).at[pl.ds(LAYER + low, -low), :], xe.at[pl.ds(low - origin, -low), :])
-        )
+        parts.append((pl.ds(LAYER + low, -low), pl.ds(low - origin, -low)))
     if high > voxels:
-        copies.append(
-            (
-                halos.pop(0).at[pl.ds(0, high - voxels), :],
-                xe.at[pl.ds(voxels - origin, high - voxels), :],
-            )
-        )
+        parts.append((pl.ds(0, high - voxels), pl.ds(voxels - origin, high - voxels)))
+    for halo, (rows, to) in zip(halos, parts):
+        for side in range(2):
+            lanes = pl.ds(side * channels, channels)
+            copies.append((halo.at[side, rows, :], xe.at[to, lanes]))
     early = len(copies)
-    copies.append((w_hbm, w_ref) if make_wt else (wt_hbm, wt))
+    copies.append((wt_hbm, wt))
     copies = [
         pltpu.make_async_copy(source, target, sems.at[i])
         for i, (source, target) in enumerate(copies)
@@ -303,11 +376,6 @@
         if chunk == 0:
             for copy in copies[early:]:
                 copy.wait()
-            if make_wt:
-                for k in range(27):
-                    span = slice(k * T, (k + 1) * T)
-                    wt[0:channels, span] = w_ref[span, :].T
-                    wt[channels:, span] = w_ref[(26 - k) * T : (27 - k) * T, :]
         pending = product(chunk)
     for _ in pending:
         pass
@@ -315,30 +383,21 @@
         copy.wait()
 
 
-def conv_run(feats, grads, low, high, neigh, weight, run, earlier, name):
+def conv_run(feats, grads, low, high, neigh, turned, run, earlier, name):
     voxels, channels = feats.shape
     out = jax.ShapeDtypeStruct((voxels, channels), jnp.bfloat16)
-    turned = jax.ShapeDtypeStruct((2 * channels, 27 * channels), jnp.bfloat16)
-    make_wt = earlier is None
-    operands = [feats, grads, neigh, weight]
-    if not make_wt:
-        conv_out, grad_in, wt = earlier
-        operands += [wt, conv_out, grad_in]
     first, end = rows_needed(run)
-    if first < 0:
-        operands.append(low)
-    if end > voxels:
-        operands.append(high)
-    hbm = pl.BlockSpec(memory_space=pltpu.HBM)
+    halos = ((low,) if first < 0 else ()) + ((high,) if end > voxels else ())
+    operands = (feats, grads, neigh, turned) + halos + earlier
     size = run[1] - run[0]
-    results = pl.pallas_call(
-        functools.partial(conv_kernel, voxels, run, make_wt),
-        out_shape=(out, out) + ((turned,) if make_wt else ()),
-        in_specs=[hbm] * len(operands),
-        out_specs=(hbm, hbm) + ((VMEM,) if make_wt else ()),
-        input_output_aliases={} if make_wt else {5: 0, 6: 1},
+    return pl.pallas_call(
+        functools.partial(conv_kernel, voxels, run, len(halos)),
+        out_shape=(out, out),
+        in_specs=[HBM] * len(operands),
+        out_specs=(HBM, HBM),
+        input_output_aliases={4 + len(halos) + i: i for i in range(len(earlier))},
         scratch_shapes=[
-            pltpu.VMEM(weight.shape if make_wt else turned.shape, jnp.bfloat16),
+            pltpu.VMEM(turned.shape, jnp.bfloat16),
             pltpu.VMEM((size, channels), jnp.bfloat16),
             pltpu.VMEM((size, channels), jnp.bfloat16),
             pltpu.VMEM((size + 2 * (LAYER + ROW), 2 * channels), jnp.bfloat16),
@@ -347,11 +406,10 @@
         ]
         + [pltpu.VMEM((27 * T, CHUNK_C), jnp.bfloat16)] * 4
         + [pltpu.SemaphoreType.DMA((8 + 2 * size // CHUNK_C,))],
-        compiler_params=pltpu.CompilerParams(vmem_limit_bytes=CONV_VMEM_LIMIT),
+        compiler_params=pltpu.CompilerParams(vmem_limit_bytes=FULL_VMEM_LIMIT),
         cost_estimate=pl.CostEstimate(flops=10**10, bytes_accessed=6 * 10**6, transcendentals=0),
         name=name,
     )(*operands)
-    return tuple(results) if make_wt else (results[0], results[1], wt)
 
 
 def sum_kernel(*refs):
@@ -408,37 +466,35 @@
     space, dp = lax.axis_size("space"), lax.axis_size("dp")
     up = [(i, i + 1) for i in range(space - 1)]
     down = [(i + 1, i) for i in range(space - 1)]
-    last = jnp.concatenate([feats[voxels - LAYER :], grads[voxels - LAYER :]], axis=1)
-    first = jnp.concatenate([feats[:LAYER], grads[:LAYER]], axis=1)
+    last, first = stack_edges(feats, grads)
     low = lax.ppermute(last, "space", up)
     high = lax.ppermute(first, "space", down)
 
     scale = 1.0 / math.sqrt(dp * space * voxels)
     share = -(-27 * channels // (16 * dp)) * 16
     parity = (lax.axis_index("dp") % 2).astype(jnp.int32).reshape(1)
-    inner = grad_w_inner(feats, grads, neigh)
+    inner, turned = grad_w_inner(feats, grads, neigh, weight.reshape(27 * channels, channels))
+    low, high, inner = lax.optimization_barrier((low, high, inner))
     mine, other = grad_w_halo(feats, grads, low, neigh, inner, parity, scale, share * dp)
     swap = [(i, i ^ 1) for i in range(dp)]
     alike = [list(range(0, dp, 2)), list(range(1, dp, 2))]
     other = lax.ppermute(other, "dp", swap)
     mine = sum_parts((mine[None], other[None]), 1, "sum_of_pair")
-    mine, flat_weight = lax.optimization_barrier(
-        (mine, weight.reshape(27 * channels, channels))
-    )
+    mine, turned = lax.optimization_barrier((mine, turned))
     chunks = voxels // CHUNK_C
-    ends = [0, chunks // 4 * CHUNK_C, chunks * 2 // 3 * CHUNK_C, voxels]
+    ends = [0, chunks // 4 * CHUNK_C, chunks * 3 // 4 * CHUNK_C, voxels]
 
     def conv(done, part):
         run = (ends[part], ends[part + 1])
         name = "conv_run_%d" % part
-        return conv_run(feats, grads, low, high, neigh, flat_weight, run, done, name)
+        return conv_run(feats, grads, low, high, neigh, turned, run, done, name)
 
     def exchange(pieces):
         return lax.all_to_all(pieces, "dp", 0, 0, axis_index_groups=alike, tiled=True)
 
     pieces = exchange(mine.reshape(dp // 2, share, channels))
-    done = conv(None, 0)
-    pieces, done, high = lax.optimization_barrier((pieces, done, high))
+    done = conv((), 0)
+    pieces, done = lax.optimization_barrier((pieces, done))
     pieces = lax.all_to_all(sum_parts((pieces,), space, "sum_for_space"), "space", 0, 0, tiled=True)
     done = conv(done, 1)
     pieces, done = lax.optimization_barrier((pieces, done))
@@ -449,7 +505,7 @@
     other = lax.ppermute(mine, "dp", swap)
     grad_w = widen(mine, parity, 27 * channels, (), "widen_own_half")
     grad_w = widen(other, 1 - parity, 27 * channels, (grad_w,), "widen_other_half")
-    conv_out, grad_in, _ = done
+    conv_out, grad_in = done
     return conv_out[None], grad_in[None], grad_w.reshape(27, channels, channels)
 
 

time: 74.1 us -> 72.2 us (0.974)
  other arithmetic: 0.91 us -> 0 us
    all_to_all x1, waiting for transfers between devices: 3.01 us -> 1.15 us  [local(): lax.all_to_all(sum_parts((pieces,), space, 'sum_for_space'), 'space', 0,...]
    ppermute x1, waiting for transfers between devices: 1.46 us -> 0.01 us  [local(): low = lax.ppermute(last, 'space', up)]
    slice x1 -> x0, local copies, waits for them, and re-layouts: 1.39 us -> none  [local(): first = jnp.concatenate([feats[:LAYER], grads[:LAYER]], axis=1)]
    ppermute x1, waiting for transfers between devices: 0.41 us -> 1.78 us  [local(): other = lax.ppermute(other, 'dp', swap)]
    unnamed x10 -> x12, local copies, waits for them, and re-layouts: 0.03 us -> 1.23 us
    pallas_call x3 -> x4, Pallas kernels: 26.4 us -> 27.5 us  [the longest x3 25.2 us: conv_run(): pl.pallas_call(functools.partial(conv_kernel, voxels, run, len(halos)), o...]
    concatenate x2 -> x0, other arithmetic: 0.91 us -> none  [the longest x1 0.85 us: local(): jnp.concatenate([feats[voxels - LAYER:], grads[voxels - LAYER:]], axis=1)]
    ppermute x1, waiting for transfers between devices: 2.34 us -> 3.13 us  [local(): high = lax.ppermute(first, 'space', down)]
  transfers between devices with their start and end apart: 7 -> 7, of which waited for: 5 -> 5; matrix products, arithmetic and copies ran while one was open for 0% -> 0% of each run, Pallas kernels for 52% -> 50%
where the time goes in v1:
time: 72.2 us; the launch traced here: 71.8 us
  Pallas kernels  44.7 us (62%)
  starting transfers between devices  17.7 us (25%)
  waiting for transfers between devices  7.39 us (10%)
  local copies, waits for them, and re-layouts  1.23 us (2%)
  between operations  0.81 us (1%)
    pallas_call x3, Pallas kernels, conv_run(): pl.pallas_call(functools.partial(conv_kernel, voxels, run, len(halos)), o...  25.2 us
    pallas_call x1, Pallas kernels, grad_w_inner(): pl.pallas_call(functools.partial(weight_inner_kernel, voxels), out_shape=...  9.89 us
    all_to_all x2, starting transfers between devices, exchange(): lax.all_to_all(pieces, 'dp', 0, 0, axis_index_groups=alike, tiled=True)  7.43 us
    ppermute x1, starting transfers between devices, local(): low = lax.ppermute(last, 'space', up)  4.95 us
    all_to_all x1, starting transfers between devices, local(): lax.all_to_all(sum_parts((pieces,), space, 'sum_for_space'), 'space', 0,...  3.84 us
    ppermute x1, waiting for transfers between devices, local(): high = lax.ppermute(first, 'space', down)  3.13 us
    pallas_call x1, Pallas kernels, grad_w_halo(): pl.pallas_call(functools.partial(weight_halo_kernel, scale), out_shape=(o...  2.87 us
    pallas_call x3, Pallas kernels, sum_parts(): pl.pallas_call(sum_kernel, out_shape=jax.ShapeDtypeStruct((copies,) + sha...  2.56 us
  transfers between devices with their start and end apart: 7, of which 5 were waited for; matrix products, arithmetic and copies ran while one was open for 0% of the time, Pallas kernels for 50%

profile of v1, /device:TPU:0, one launch (start us, length us, event | category | flops | bytes accessed | tf_op | source)
XLA Modules:
  0.0 71.8 jit_solution(9047535806331823820)
XLA Ops:
  0.6 0.0 copy-start
  0.6 0.0 copy-start.1
  0.7 0.0 copy-start.4
  0.7 0.0 copy-start.2
  0.7 2.3 %stack_edges.1 = (bf16[2,1024,128]{2,1,0:T(8,128)(2,1)}, bf16[2,1024,128]{2,1,0:T(8,128)(2,1)}) custom-call(bf16[3072,128]{1,0:T(8,128)(2,1)} %bitcast.12, bf16[3072,128]{1,0:T(8,128)(2,1)} %bitcast.19, bf16[3072,128]{1,0:T(8,128)(2,1)} %bitcast.13, bf16[3072,128]{1,0:T(8,128)(2,1)} %bitcast.20), custom_call_target="tpu_custom_call" | custom-call | tf_op jit(solution)/shard_map/stack_edges/pallas_call | solution.py:232
  3.0 4.9 %collective-permute-start = (bf16[2,1024,128]{2,1,0:T(8,128)(2,1)}, bf16[2,1024,128]{2,1,0:T(8,128)(2,1)S(1)}, u32[]{:S(2)}, u32[]{:S(2)}) collective-permute-start(bf16[2,1024,128]{2,1,0:T(8,128)(2,1)} %get-tuple-element.29), channel_id=1, source_target_pairs={{0,1},{1,2},{2,3},{4,5},{5,6},{6,7},{8,9},{9,10},{10,11},{12,13},{... | collective-permute-start | bytes 1572872 | tf_op jit(solution)/shard_map/ppermute | solution.py:470
  8.0 1.3 %collective-permute-start.1 = (bf16[2,1024,128]{2,1,0:T(8,128)(2,1)}, bf16[2,1024,128]{2,1,0:T(8,128)(2,1)}, u32[]{:S(2)}, u32[]{:S(2)}) collective-permute-start(bf16[2,1024,128]{2,1,0:T(8,128)(2,1)} %get-tuple-element.30), channel_id=1, source_target_pairs={{1,0},{2,1},{3,2},{5,4},{6,5},{7,6},{9,8},{10,9},{11,10},{13,12},{... | collective-permute-start | bytes 1572872 | tf_op jit(solution)/shard_map/ppermute | solution.py:471
  9.3 0.0 copy-done
  9.3 0.0 copy-done.1
  9.3 0.0 copy-done.4
  9.3 0.0 copy-done.2
  9.3 9.9 %weight_gradient_inner.1 = (f32[128,3456]{1,0:T(8,128)S(1)}, bf16[256,3456]{1,0:T(8,128)(2,1)S(1)}) custom-call(bf16[3072,128]{1,0:T(8,128)(2,1)S(1)} %bitcast.17, bf16[3072,128]{1,0:T(8,128)(2,1)S(1)} %bitcast.24, s32[27,24,128]{2,1,0:T(8,128)S(1)} %bitcast.34, bf16[3456,128]{1,0:T(8,128)(2,1)S(1)} %bitcast.30), custom_call_target="tpu_custom_call" | custom-call | flops 8000000000 | bytes 4000000 | tf_op jit(solution)/shard_map/weight_gradient_inner/pallas_call | solution.py:182
  19.2 0.0 copy-start.5
  19.2 1.2 %copy-done.5 = bf16[256,3456]{1,0:T(8,128)(2,1)} copy-done((bf16[256,3456]{1,0:T(8,128)(2,1)}, bf16[256,3456]{1,0:T(8,128)(2,1)S(1)}, u32[]{:S(2)}) %copy-start.5) | copy-done | bytes 1769496
  20.4 0.0 collective-permute-done.low_ref.rest_0_
  20.4 0.0 copy-start.3
  20.4 3.1 %collective-permute-done.1.rest_1_.rest_0_ = bf16[2,1024,128]{2,1,0:T(8,128)(2,1)} collective-permute-done((bf16[2,1024,128]{2,1,0:T(8,128)(2,1)}, bf16[2,1024,128]{2,1,0:T(8,128)(2,1)}, u32[]{:S(2)}, u32[]{:S(2)}) %collective-permute-start.1) | collective-permute-done | bytes 524320 | tf_op jit(solution)/shard_map/ppermute | solution.py:471
  23.6 2.9 %weight_gradient_halo.1 = (bf16[1728,128]{1,0:T(8,128)(2,1)S(1)}, bf16[1728,128]{1,0:T(8,128)(2,1)S(1)}) custom-call(s32[1]{0:T(128)} %bitcast.parity_ref.side_ref, bf16[3072,128]{1,0:T(8,128)(2,1)S(1)} %bitcast.18, bf16[3072,128]{1,0:T(8,128)(2,1)S(1)} %bitcast.25, bf16[2,1024,128]{2,1,0:T(8,128)(2,1)S(1)} %collective-permute-done.low_ref.rest_0_, ...), custom_call_target="tpu_custom_call" | custom-call | flops 3000000000 | bytes 4000000 | tf_op jit(solution)/shard_map/weight_gradient_halo/pallas_call | solution.py:203
  26.4 0.0 copy-done.3
  26.5 0.1 collective-permute-start.2
  26.5 1.8 %collective-permute-done.2 = bf16[1728,128]{1,0:T(8,128)(2,1)S(1)} collective-permute-done((bf16[1728,128]{1,0:T(8,128)(2,1)S(1)}, bf16[1728,128]{1,0:T(8,128)(2,1)S(1)}, u32[]{:S(2)}, u32[]{:S(2)}) %collective-permute-start.2) | collective-permute-done | bytes 442400 | tf_op jit(solution)/shard_map/ppermute | solution.py:481
  28.3 0.9 %sum_of_pair.1 = bf16[1,1728,128]{2,1,0:T(8,128)(2,1)} custom-call(bf16[1,1728,128]{2,1,0:T(8,128)(2,1)S(1)} %bitcast.28, bf16[1,1728,128]{2,1,0:T(8,128)(2,1)S(1)} %bitcast.29), custom_call_target="tpu_custom_call" | custom-call | tf_op jit(solution)/shard_map/sum_of_pair/pallas_call | solution.py:428
  29.2 3.7 %all-to-all-start = ((bf16[4,432,128]{2,1,0:T(8,128)(2,1)}), bf16[4,432,128]{2,1,0:T(8,128)(2,1)S(1)}, u32[]{:S(2)}, u32[]{:S(2)}) async-start(bf16[4,432,128]{2,1,0:T(8,128)(2,1)} %bitcast.7), calls=%async_computation | async-start | bytes 884736 | tf_op jit(solution)/shard_map/all_to_all | solution.py:493
  32.9 6.9 %conv_run_0.1 = (bf16[3072,128]{1,0:T(8,128)(2,1)}, bf16[3072,128]{1,0:T(8,128)(2,1)}) custom-call(bf16[3072,128]{1,0:T(8,128)(2,1)} %bitcast.14, bf16[3072,128]{1,0:T(8,128)(2,1)} %bitcast.21, s32[27,24,128]{2,1,0:T(8,128)} %bitcast.31, bf16[256,3456]{1,0:T(8,128)(2,1)} %copy-done.5, bf16[2,1024,128]{2,1,0:T(8,128)(2,1)} %copy-done.3), custom_call_target="tpu_custom_call" | custom-call | flops 10000000000 | bytes 6000000 | tf_op jit(solution)/shard_map/conv_run_0/pallas_call | solution.py:393
  39.8 0.5 all-to-all-done.refs_0_
  40.4 0.8 %sum_for_space.1 = bf16[4,432,128]{2,1,0:T(8,128)(2,1)} custom-call(bf16[4,432,128]{2,1,0:T(8,128)(2,1)S(1)} %all-to-all-done.refs_0_), custom_call_target="tpu_custom_call" | custom-call | tf_op jit(solution)/shard_map/sum_for_space/pallas_call | solution.py:428
  41.2 3.8 %all-to-all-start.1 = ((bf16[4,432,128]{2,1,0:T(8,128)(2,1)}), bf16[4,432,128]{2,1,0:T(8,128)(2,1)S(1)}, u32[]{:S(2)}, u32[]{:S(2)}) async-start(bf16[4,432,128]{2,1,0:T(8,128)(2,1)} %sum_for_space.1), calls=%async_computation.1 | async-start | bytes 884736 | tf_op jit(solution)/shard_map/all_to_all | solution.py:498
  45.0 11.3 %conv_run_1.1 = (bf16[3072,128]{1,0:T(8,128)(2,1)}, bf16[3072,128]{1,0:T(8,128)(2,1)}) custom-call(bf16[3072,128]{1,0:T(8,128)(2,1)} %bitcast.15, bf16[3072,128]{1,0:T(8,128)(2,1)} %bitcast.22, s32[27,24,128]{2,1,0:T(8,128)} %bitcast.32, bf16[256,3456]{1,0:T(8,128)(2,1)} %copy-done.5, ...), custom_call_target="tpu_custom_call", output_to_operand_aliasing={{0}: (6, {}), {1}: (7, {})} | custom-call | flops 10000000000 | bytes 6000000 | tf_op jit(solution)/shard_map/conv_run_1/pallas_call | solution.py:393
  56.4 1.1 %all-to-all-done.1.refs_0_ = bf16[4,432,128]{2,1,0:T(8,128)(2,1)S(1)} async-done(((bf16[4,432,128]{2,1,0:T(8,128)(2,1)}), bf16[4,432,128]{2,1,0:T(8,128)(2,1)S(1)}, u32[]{:S(2)}, u32[]{:S(2)}) %all-to-all-start.1) | async-done | bytes 442400 | tf_op jit(solution)/shard_map/all_to_all | solution.py:498
  57.5 0.8 %sum_for_dp.1 = bf16[4,432,128]{2,1,0:T(8,128)(2,1)} custom-call(bf16[4,432,128]{2,1,0:T(8,128)(2,1)S(1)} %all-to-all-done.1.refs_0_), custom_call_target="tpu_custom_call" | custom-call | tf_op jit(solution)/shard_map/sum_for_dp/pallas_call | solution.py:428
  58.3 3.7 %all-to-all-start.2 = ((bf16[4,432,128]{2,1,0:T(8,128)(2,1)}), bf16[4,432,128]{2,1,0:T(8,128)(2,1)S(1)}, u32[]{:S(2)}, u32[]{:S(2)}) async-start(bf16[4,432,128]{2,1,0:T(8,128)(2,1)} %sum_for_dp.1), calls=%async_computation.2 | async-start | bytes 884736 | tf_op jit(solution)/shard_map/all_to_all | solution.py:493
  62.1 6.9 %conv_run_2.1 = (bf16[3072,128]{1,0:T(8,128)(2,1)}, bf16[3072,128]{1,0:T(8,128)(2,1)}) custom-call(bf16[3072,128]{1,0:T(8,128)(2,1)} %bitcast.16, bf16[3072,128]{1,0:T(8,128)(2,1)} %bitcast.23, s32[27,24,128]{2,1,0:T(8,128)} %bitcast.33, bf16[256,3456]{1,0:T(8,128)(2,1)} %copy-done.5, ...), custom_call_target="tpu_custom_call", output_to_operand_aliasing={{0}: (5, {}), {1}: (6, {})} | custom-call | flops 10000000000 | bytes 6000000 | tf_op jit(solution)/shard_map/conv_run_2/pallas_call | solution.py:393
  69.0 0.0 all-to-all-done.2
  69.0 0.1 collective-permute-start.3
  69.1 1.0 %widen_own_half.1.rest_0_ = f32[3456,128]{1,0:T(8,128)} custom-call(s32[1]{0:T(128)} %bitcast.parity_ref.side_ref, bf16[1728,128]{1,0:T(8,128)(2,1)S(1)} %bitcast.27), custom_call_target="tpu_custom_call" | custom-call | tf_op jit(solution)/shard_map/widen_own_half/pallas_call | solution.py:446
  70.0 0.8 %collective-permute-done.3.in_ref = bf16[1728,128]{1,0:T(8,128)(2,1)S(1)} collective-permute-done((bf16[1728,128]{1,0:T(8,128)(2,1)S(1)}, bf16[1728,128]{1,0:T(8,128)(2,1)S(1)}, u32[]{:S(2)}, u32[]{:S(2)}) %collective-permute-start.3) | collective-permute-done | bytes 442400 | tf_op jit(solution)/shard_map/ppermute | solution.py:505
  70.9 0.9 %widen_other_half.1 = f32[3456,128]{1,0:T(8,128)} custom-call(s32[1]{0:T(128)S(6)} %sub.3.side_ref, bf16[1728,128]{1,0:T(8,128)(2,1)S(1)} %collective-permute-done.3.in_ref, f32[3456,128]{1,0:T(8,128)} %widen_own_half.1.rest_0_), custom_call_target="tpu_custom_call", output_to_operand_aliasing={{}: (2, {})} | custom-call | tf_op jit(solution)/shard_map/widen_other_half/pallas_call | solution.py:446
Async XLA Ops:
  0.6 8.7 %copy-start = (bf16[1,3072,128]{2,1,0:T(8,128)(2,1)S(1)}, bf16[1,3072,128]{2,1,0:T(8,128)(2,1)}, u32[]{:S(2)}) copy-start(bf16[1,3072,128]{2,1,0:T(8,128)(2,1)} %param.4) | copy-start | bytes 2359300
  0.6 8.7 %copy-start.1 = (bf16[1,3072,128]{2,1,0:T(8,128)(2,1)S(1)}, bf16[1,3072,128]{2,1,0:T(8,128)(2,1)}, u32[]{:S(2)}) copy-start(bf16[1,3072,128]{2,1,0:T(8,128)(2,1)} %param.7) | copy-start | bytes 2359300
  0.7 8.7 %copy-start.4 = (s32[1,27,3072]{2,0,1:T(1,128)S(1)}, s32[1,27,3072]{2,0,1:T(1,128)}, u32[]{:S(2)}) copy-start(s32[1,27,3072]{2,0,1:T(1,128)} %param.5) | copy-start | bytes 995332
  0.7 8.6 %copy-start.2 = (bf16[27,128,128]{2,1,0:T(8,128)(2,1)S(1)}, bf16[27,128,128]{2,1,0:T(8,128)(2,1)}, u32[]{:S(2)}) copy-start(bf16[27,128,128]{2,1,0:T(8,128)(2,1)} %param.6) | copy-start | bytes 2654212
  3.0 17.4 %collective-permute-start = (bf16[2,1024,128]{2,1,0:T(8,128)(2,1)}, bf16[2,1024,128]{2,1,0:T(8,128)(2,1)S(1)}, u32[]{:S(2)}, u32[]{:S(2)}) collective-permute-start(bf16[2,1024,128]{2,1,0:T(8,128)(2,1)} %get-tuple-element.29), channel_id=1, source_target_pairs={{0,1},{1,2},{2,3},{4,5},{5,6},{6,7},{8,9},{9,10},{10,11},{12,13},{... | collective-permute-start | bytes 1572872 | tf_op jit(solution)/shard_map/ppermute | solution.py:470
  8.0 15.6 %collective-permute-start.1 = (bf16[2,1024,128]{2,1,0:T(8,128)(2,1)}, bf16[2,1024,128]{2,1,0:T(8,128)(2,1)}, u32[]{:S(2)}, u32[]{:S(2)}) collective-permute-start(bf16[2,1024,128]{2,1,0:T(8,128)(2,1)} %get-tuple-element.30), channel_id=1, source_target_pairs={{1,0},{2,1},{3,2},{5,4},{6,5},{7,6},{9,8},{10,9},{11,10},{13,12},{... | collective-permute-start | bytes 1572872 | tf_op jit(solution)/shard_map/ppermute | solution.py:471
  19.2 1.2 %copy-start.5 = (bf16[256,3456]{1,0:T(8,128)(2,1)}, bf16[256,3456]{1,0:T(8,128)(2,1)S(1)}, u32[]{:S(2)}) copy-start(bf16[256,3456]{1,0:T(8,128)(2,1)S(1)} %get-tuple-element.38.wt_hbm) | copy-start | bytes 5308420
  20.4 6.0 %copy-start.3 = (bf16[2,1024,128]{2,1,0:T(8,128)(2,1)}, bf16[2,1024,128]{2,1,0:T(8,128)(2,1)S(1)}, u32[]{:S(2)}) copy-start(bf16[2,1024,128]{2,1,0:T(8,128)(2,1)S(1)} %collective-permute-done.low_ref.rest_0_) | copy-start | bytes 1572868
  26.5 1.9 %collective-permute-start.2 = (bf16[1728,128]{1,0:T(8,128)(2,1)S(1)}, bf16[1728,128]{1,0:T(8,128)(2,1)S(1)}, u32[]{:S(2)}, u32[]{:S(2)}) collective-permute-start(bf16[1728,128]{1,0:T(8,128)(2,1)S(1)} %get-tuple-element.35), channel_id=1, source_target_pairs={{0,4},{4,0},{8,12},{12,8},{16,20},{20,16},{24,28},{28,24},{1,5},{5... | collective-permute-start | bytes 1327112 | tf_op jit(solution)/shard_map/ppermute | solution.py:481
  29.2 11.2 %all-to-all-start = ((bf16[4,432,128]{2,1,0:T(8,128)(2,1)}), bf16[4,432,128]{2,1,0:T(8,128)(2,1)S(1)}, u32[]{:S(2)}, u32[]{:S(2)}) async-start(bf16[4,432,128]{2,1,0:T(8,128)(2,1)} %bitcast.7), calls=%async_computation | async-start | bytes 884736 | tf_op jit(solution)/shard_map/all_to_all | solution.py:493
  41.2 16.3 %all-to-all-start.1 = ((bf16[4,432,128]{2,1,0:T(8,128)(2,1)}), bf16[4,432,128]{2,1,0:T(8,128)(2,1)S(1)}, u32[]{:S(2)}, u32[]{:S(2)}) async-start(bf16[4,432,128]{2,1,0:T(8,128)(2,1)} %sum_for_space.1), calls=%async_computation.1 | async-start | bytes 884736 | tf_op jit(solution)/shard_map/all_to_all | solution.py:498
  58.3 10.7 %all-to-all-start.2 = ((bf16[4,432,128]{2,1,0:T(8,128)(2,1)}), bf16[4,432,128]{2,1,0:T(8,128)(2,1)S(1)}, u32[]{:S(2)}, u32[]{:S(2)}) async-start(bf16[4,432,128]{2,1,0:T(8,128)(2,1)} %sum_for_dp.1), calls=%async_computation.2 | async-start | bytes 884736 | tf_op jit(solution)/shard_map/all_to_all | solution.py:493
  69.0 1.9 %collective-permute-start.3 = (bf16[1728,128]{1,0:T(8,128)(2,1)S(1)}, bf16[1728,128]{1,0:T(8,128)(2,1)S(1)}, u32[]{:S(2)}, u32[]{:S(2)}) collective-permute-start(bf16[1728,128]{1,0:T(8,128)(2,1)S(1)} %bitcast.26), channel_id=1, source_target_pairs={{0,4},{4,0},{8,12},{12,8},{16,20},{20,16},{24,28},{28,24},{1,5},{5... | collective-permute-start | bytes 1327112 | tf_op jit(solution)/shard_map/ppermute | solution.py:505
